TPU v7x, 32 devices: a whole 2x2x4 slice. The times are simulated.
32 devices in a mesh: groups: 2 (over x), seq: 16 (over z, y, core).
Axes of the slice: x: 2, y: 2, z: 4, core: 2. Of those that a mesh axis runs over, the one named last changes fastest.
Arguments:
- queries: bfloat16 [16384, 2048], P(('groups', 'seq')), parts along dimension 0, may hold values from -8 to 8
- keys: bfloat16 [16384, 512], P(('groups', 'seq')), parts along dimension 0, may hold values from -8 to 8
- values: bfloat16 [16384, 512], P(('groups', 'seq')), parts along dimension 0, may hold values from -6 to 6
- block_table: int32 [128, 8], P(('groups', 'seq')), parts along dimension 0, may hold values from 0 to 63, as said below
- out_weight: bfloat16 [2048, 4096], P('seq'), may hold values from -0.125 to 0.125
Outputs:
- projected: bfloat16 [16384, 4096], P(('groups', 'seq')), parts along dimension 0
There are 2 independent parts, one for each index of `groups`. A program takes and returns all parts, laid end to end along the dimension named above; an argument that names none is the same for every part. Nothing has to cross between parts.
Inputs may be any that keep to these rules, and one draw needn't show every extreme that they name: `block_table`: entry j of the row of query block b names a key block held by index (b // 4 + j * 2 - ((b mod 4) mod 2)) mod 16 of seq, that is a block number s * 4 + r with that index s and 0 <= r < 4.
All inputs are finite; a program needn't handle non-finite values.
Results may differ from a plain program's by a relative error of at most 0.013.
Values may be sent and summed in bfloat16 or wider, within the bound.
A program may use at most 320 MiB of HBM per device.

v0:
```python
import functools

import jax
import jax.numpy as jnp
from jax import lax
from jax.experimental import pallas as pl
from jax.experimental.pallas import tpu as pltpu
from jax.sharding import PartitionSpec as P

H = 16
KVH = 4
HD = 128
QB = 128
ENTRIES = 8
MESH = pl.DeviceIdType.MESH
LOG2E = 1.4426950408889634


def kernel(
    Z, Y, q_ref, k_ref, v_ref, t_ref, w_ref, o_ref,
    q_all, kv, t_all, t_smem, w_all, att, att_full, send, recv, local,
):
    cell = 2 * Y
    hp = KVH // cell
    gh = H // KVH
    tok = q_ref.shape[0]
    nq = tok // QB
    wrows = w_ref.shape[0]
    half = wrows // 2
    qc = hp * gh * HD
    kc = hp * HD

    g = lax.axis_index("groups")
    s = lax.axis_index("seq")
    z = lax.div(s, cell)
    i = lax.rem(s, cell)
    y = lax.div(i, 2)
    c = lax.rem(i, 2)
    xh = lax.rem(g, 2)
    gx = g + 1 - 2 * xh

    def dev(dy, dc):
        yy = 1 - y if dy else y
        cc = 1 - c if dc else c
        return yy * 2 + cc

    cores = i - c + (1 - c)
    partners = [dev(dy, dc) for dy in range(Y - 1, -1, -1) for dc in (1, 0) if dy or dc]
    has_left = z > 0
    has_right = z < Z - 1

    counter = [0]

    def new_id():
        counter[0] += 1
        return counter[0] - 1

    def rcopy(n, src, dst, gg, ss):
        return pltpu.make_async_remote_copy(
            src_ref=src, dst_ref=dst, send_sem=send.at[n], recv_sem=recv.at[n],
            device_id=(gg, ss), device_id_type=MESH,
        )

    pending = []

    barrier = pltpu.get_barrier_semaphore()
    for p in partners:
        pl.semaphore_signal(barrier, inc=1, device_id=(g, z * cell + p), device_id_type=MESH)
    pl.semaphore_signal(barrier, inc=1, device_id=(gx, s), device_id_type=MESH)

    @pl.when(has_left)
    def _():
        pl.semaphore_signal(barrier, inc=1, device_id=(g, s - cell), device_id_type=MESH)

    @pl.when(has_right)
    def _():
        pl.semaphore_signal(barrier, inc=1, device_id=(g, s + cell), device_id_type=MESH)

    edges = jnp.where(has_left, 1, 0) + jnp.where(has_right, 1, 0)
    pl.semaphore_wait(barrier, len(partners) + 1 + edges)

    def wunit(origin, idx, xx, rows=None):
        start = (origin * cell + idx) * wrows + xx * half
        return w_all.at[pl.ds(pl.multiple_of(start, 16), half), :]

    def wpair(origin, idx):
        start = (origin * cell + idx) * wrows
        return w_all.at[pl.ds(pl.multiple_of(start, 16), wrows), :]

    def layer_rows(origin):
        n = cell * nq
        return kv.at[:, pl.ds(origin * n, n)]

    def z_copies(ids, src_of, dst_of, t):
        right = (has_right & (z - t >= 0), lambda: rcopy(ids[0], src_of(z - t), dst_of(z - t), g, s + cell))
        left = (has_left & (z + t <= Z - 1), lambda: rcopy(ids[1], src_of(z + t), dst_of(z + t), g, s - cell))
        from_left = (z - 1 - t >= 0, lambda: rcopy(ids[0], dst_of(z - 1 - t), dst_of(z - 1 - t), g, s + cell))
        from_right = (z + 1 + t <= Z - 1, lambda: rcopy(ids[1], dst_of(z + 1 + t), dst_of(z + 1 + t), g, s - cell))
        return (right, left), (from_left, from_right)

    def start_if(cond, make):
        @pl.when(cond)
        def _():
            make().start()

        pending.append((cond, make))

    def start(make):
        make().start()
        pending.append((None, make))

    def wait_recv_if(cond, make):
        @pl.when(cond)
        def _():
            make().wait_recv()

    loc = [
        pltpu.make_async_copy(k_ref.at[:, :, pl.ds(pl.multiple_of(i * kc, 128), kc)],
                              kv.at[0, pl.ds(s * nq, nq)], local.at[0]),
        pltpu.make_async_copy(v_ref.at[:, :, pl.ds(pl.multiple_of(i * kc, 128), kc)],
                              kv.at[1, pl.ds(s * nq, nq)], local.at[1]),
        pltpu.make_async_copy(q_ref.at[:, pl.ds(pl.multiple_of(i * qc, 128), qc)],
                              q_all.at[pl.ds(pl.multiple_of(i * tok, 128), tok), :], local.at[2]),
        pltpu.make_async_copy(t_ref, t_all.at[i], local.at[3]),
        pltpu.make_async_copy(w_ref, wpair(z, i), local.at[4]),
    ]
    for cp in loc:
        cp.start()

    def w_src0(origin):
        return w_ref.at[pl.ds(pl.multiple_of(xh * half, 16), half), :]

    wz_ids = [(new_id(), new_id()) for _ in range(Z - 1)]
    kz_ids = [(new_id(), new_id()) for _ in range(Z - 1)]

    def wz(t):
        if t == 0:
            dst = lambda origin: wunit(origin, i, xh)
            return z_copies(wz_ids[0], w_src0, dst, 0)
        same = lambda origin: wunit(origin, i, xh)
        return z_copies(wz_ids[t], same, same, t)

    def kz(t):
        return z_copies(kz_ids[t], layer_rows, layer_rows, t)

    for cond, make in wz(0)[0]:
        start_if(cond, make)

    kv_in, q_in, t_in = [], [], []
    for p in partners:
        for which, ref in ((0, k_ref), (1, v_ref)):
            n = new_id()

            def make(n=n, p=p, which=which, ref=ref):
                return rcopy(n, ref.at[:, :, pl.ds(pl.multiple_of(p * kc, 128), kc)],
                             kv.at[which, pl.ds(s * nq, nq)], g, z * cell + p)

            def landed(n=n, p=p, which=which):
                at = kv.at[which, pl.ds((z * cell + p) * nq, nq)]
                return rcopy(n, at, at, g, z * cell + p)

            start(make)
            kv_in.append(landed)
    def w_send(make_src, make_dst, gg, ss, make_land, cond=None):
        n = new_id()
        make = lambda: rcopy(n, make_src(), make_dst(), gg, ss)
        if cond is None:
            start(make)
        else:
            start_if(cond, make)
        return (cond, lambda: rcopy(n, make_land(), make_land(), gg, ss))

    yi = (1 - y) * 2 + c
    core_dev = z * cell + cores
    y_dev = z * cell + yi
    y_cores = (1 - y) * 2 + (1 - c)

    def send_core(origin, idx, xx, idx_there, xx_there, cond=None):
        return w_send(lambda: wunit(origin, idx, xx), lambda: wunit(origin, idx, xx), g, core_dev,
                      lambda: wunit(origin, idx_there, xx_there), cond)

    final = []
    n_own = new_id()
    own_core = lambda: rcopy(n_own, w_ref, wpair(z, i), g, core_dev)
    start(own_core)
    final.append((None, lambda: rcopy(n_own, wpair(z, cores), wpair(z, cores), g, core_dev)))
    y_lands = []
    if Y == 2:
        y_lands.append((z, None, w_send(lambda: w_src0(z), lambda: wunit(z, i, xh), g, y_dev,
                                        lambda: wunit(z, yi, xh))))
    for p in partners:
        n = new_id()

        def make(n=n, p=p):
            return rcopy(n, q_ref.at[:, pl.ds(pl.multiple_of(p * qc, 128), qc)],
                         q_all.at[pl.ds(pl.multiple_of(i * tok, 128), tok), :], g, z * cell + p)

        def landed(n=n, p=p):
            at = q_all.at[pl.ds(pl.multiple_of(p * tok, 128), tok), :]
            return rcopy(n, at, at, g, z * cell + p)

        start(make)
        q_in.append(landed)
        m = new_id()

        def make_t(m=m, p=p):
            return rcopy(m, t_ref, t_all.at[i], g, z * cell + p)

        def landed_t(m=m, p=p):
            return rcopy(m, t_all.at[p], t_all.at[p], g, z * cell + p)

        start(make_t)
        q_in.append(landed_t)

    x_lands = []

    def spread(origin, cond):
        x_lands.append((origin, cond, i, w_send(
            lambda: wunit(origin, i, xh), lambda: wunit(origin, i, xh), gx, s,
            lambda: wunit(origin, i, 1 - xh), cond)))
        if Y == 2:
            y_lands.append((origin, cond, w_send(
                lambda: wunit(origin, i, xh), lambda: wunit(origin, i, xh), g, y_dev,
                lambda: wunit(origin, yi, xh), cond)))
        final.append(send_core(origin, i, xh, cores, xh, cond))

    def maybe_wait(entry):
        cond, make = entry
        if cond is None:
            make().wait_recv()
        else:
            wait_recv_if(cond, make)

    def relay_y():
        while y_lands:
            origin, cond, entry = y_lands.pop(0)
            maybe_wait(entry)
            x_lands.append((origin, cond, yi, w_send(
                lambda origin=origin: wunit(origin, yi, xh), lambda origin=origin: wunit(origin, yi, xh), gx, s,
                lambda origin=origin: wunit(origin, yi, 1 - xh), cond)))
            final.append(send_core(origin, yi, xh, y_cores, xh, cond))

    def relay_x():
        while x_lands:
            origin, cond, idx, entry = x_lands.pop(0)
            maybe_wait(entry)
            there = cores if idx is i else y_cores
            final.append(send_core(origin, idx, 1 - xh, there, 1 - xh, cond))

    def w_step(t):
        for cond, make in wz(t)[1]:
            wait_recv_if(cond, make)
        if t + 1 < Z - 1:
            for cond, make in wz(t + 1)[0]:
                start_if(cond, make)
        spread(z - 1 - t, z - 1 - t >= 0)
        spread(z + 1 + t, z + 1 + t <= Z - 1)

    def k_step(t):
        for cond, make in kz(t)[1]:
            wait_recv_if(cond, make)
        if t + 1 < Z - 1:
            for cond, make in kz(t + 1)[0]:
                start_if(cond, make)

    w_step(0)
    for make in kv_in:
        make().wait_recv()
    for cp in loc:
        cp.wait()
    for cond, make in kz(0)[0]:
        start_if(cond, make)
    for t in range(1, Z - 1):
        w_step(t)
    k_step(0)
    relay_y()
    for t in range(1, Z - 1):
        k_step(t)
    relay_x()

    for make in q_in:
        make().wait_recv()
    tcp = pltpu.make_async_copy(t_all, t_smem, local.at[5])
    tcp.start()
    tcp.wait()

    factor = HD ** -0.5 * LOG2E

    def attend(owner):
        def block(b, carry):
            rows = pl.ds(pl.multiple_of(owner * tok + b * QB, QB), QB)
            ids = [t_smem[owner, b, e] for e in range(ENTRIES)]
            for hh in range(hp):
                kcols = pl.ds(hh * HD, HD)
                keys = jnp.concatenate([kv[0, n, :, kcols] for n in ids], 0)
                vals = jnp.concatenate([kv[1, n, :, kcols] for n in ids], 0)
                for pair in range(gh // 2):
                    cols = [pl.ds((hh * gh + pair * 2 + h) * HD, HD) for h in range(2)]
                    qq = jnp.concatenate([q_all[rows, cc] for cc in cols], 0)
                    sc = lax.dot_general(qq, keys, (((1,), (1,)), ((), ())),
                                         preferred_element_type=jnp.float32)
                    top = jnp.max(sc, axis=-1, keepdims=True)
                    wts = jnp.exp2((sc - top) * factor)
                    total = jnp.sum(wts, axis=-1, keepdims=True)
                    mixed = jnp.dot(wts.astype(jnp.bfloat16), vals, preferred_element_type=jnp.float32)
                    mixed = (mixed / total).astype(jnp.bfloat16)
                    for h in range(2):
                        att[rows, cols[h]] = mixed[h * QB:(h + 1) * QB]
            return carry

        lax.fori_loop(0, nq, block, 0)

    att_in = []
    for p in partners:
        attend(p)
        n = new_id()

        def make(n=n, p=p):
            return rcopy(n, att.at[pl.ds(pl.multiple_of(p * tok, 128), tok), :],
                         att_full.at[:, pl.ds(pl.multiple_of(i * qc, 128), qc)], g, z * cell + p)

        def landed(n=n, p=p):
            at = att_full.at[:, pl.ds(pl.multiple_of(p * qc, 128), qc)]
            return rcopy(n, at, at, g, z * cell + p)

        start(make)
        att_in.append(landed)
    attend(i)
    own = pltpu.make_async_copy(att.at[pl.ds(pl.multiple_of(i * tok, 128), tok), :],
                                att_full.at[:, pl.ds(pl.multiple_of(i * qc, 128), qc)], local.at[6])
    own.start()
    own.wait()
    for make in att_in:
        make().wait_recv()
    for entry in final:
        maybe_wait(entry)

    tile = 512
    def project(j, carry):
        cols = pl.ds(pl.multiple_of(j * tile, tile), tile)
        o_ref[:, cols] = jnp.dot(att_full[...], w_all[:, cols],
                                 preferred_element_type=jnp.float32).astype(jnp.bfloat16)
        return carry

    lax.fori_loop(0, o_ref.shape[1] // tile, project, 0)
    for cond, make in pending:
        if cond is None:
            make().wait_send()
        else:
            @pl.when(cond)
            def _(make=make):
                make().wait_send()


def body(Z, Y, queries, keys, values, block_table, out_weight):
    tok, width = queries.shape
    cell = 2 * Y
    hp = KVH // cell
    D = out_weight.shape[1]
    table = jnp.pad(block_table, ((0, 8 - block_table.shape[0]), (0, 128 - ENTRIES)))
    blocks = (tok // QB, QB, KVH * HD)
    steps = Z - 1
    n_sems = steps * 4 + (cell - 1) * 5 + 8 + steps * 2 * 9
    flops = 2 * tok * width * D + 4 * tok * H * ENTRIES * QB * HD
    return pl.pallas_call(
        functools.partial(kernel, Z, Y),
        out_shape=jax.ShapeDtypeStruct((tok, D), jnp.bfloat16),
        in_specs=[pl.BlockSpec(memory_space=pl.ANY)] * 5,
        out_specs=pl.BlockSpec(memory_space=pltpu.VMEM),
        scratch_shapes=[
            pltpu.VMEM((cell * tok, width // cell), jnp.bfloat16),
            pltpu.VMEM((2, Z * cell * tok // QB, QB, hp * HD), jnp.bfloat16),
            pltpu.VMEM((cell, 8, 128), jnp.int32),
            pltpu.SMEM((cell, 8, 128), jnp.int32),
            pltpu.VMEM((out_weight.shape[0] * Z * cell, D), jnp.bfloat16),
            pltpu.VMEM((cell * tok, width // cell), jnp.bfloat16),
            pltpu.VMEM((tok, width), jnp.bfloat16),
            pltpu.SemaphoreType.DMA((n_sems,)),
            pltpu.SemaphoreType.DMA((n_sems,)),
            pltpu.SemaphoreType.DMA((7,)),
        ],
        compiler_params=pltpu.CompilerParams(
            collective_id=0, has_side_effects=True, vmem_limit_bytes=58 * 1024 * 1024,
        ),
        cost_estimate=pl.CostEstimate(flops=flops, bytes_accessed=64 * 1024 * 1024, transcendentals=0),
    )(queries, keys.reshape(blocks), values.reshape(blocks), table, out_weight)


def solution(mesh):
    groups, seq = mesh.shape["groups"], mesh.shape["seq"]
    Y = 2 if groups == 2 else 1
    Z = seq // (2 * Y)
    in_specs = (
        P(("groups", "seq"), None),
        P(("groups", "seq"), None),
        P(("groups", "seq"), None),
        P(("groups", "seq"), None),
        P("seq", None),
    )
    return jax.shard_map(
        functools.partial(body, Z, Y), mesh=mesh, in_specs=in_specs,
        out_specs=P(("groups", "seq"), None), check_vma=False,
    )
```

profile of v0, /device:TPU:0, one launch (start us, length us, event | category | flops | bytes accessed | tf_op | source)
XLA Modules:
  0.0 165.4 jit_solution(15170503723232131818)
XLA Ops:
  0.0 1.3 pad.4.t_ref
  1.3 159.4 %shard_map.55 = bf16[512,4096]{1,0:T(8,128)(2,1)} custom-call(bf16[512,2048]{1,0:T(8,128)(2,1)} %q_ref.1, bf16[4,128,512]{2,1,0:T(8,128)(2,1)} %bitcast.2, bf16[4,128,512]{2,1,0:T(8,128)(2,1)} %bitcast.3, s32[8,128]{1,0:T(8,128)} %pad.4.t_ref, bf16[128,4096]{1,0:T(8,128)(2,1)} %w_ref.1), custom_call_target="tpu_custom_call" | custom-call | flops 12884901888 | bytes 67108864 | tf_op jit(solution)/shard_map/pallas_call | solution.py:365
  160.7 4.7 %copy.7 = bf16[512,4096]{1,0:T(8,128)(2,1)} copy(bf16[512,4096]{1,0:T(8,128)(2,1)} %shard_map.55) | data formatting | bytes 8388608
where the time goes:
time: 166 us; the launch traced here: 165 us
  Pallas kernels  159 us (96%)
  local copies, waits for them, and re-layouts  5.98 us (4%)
    pallas_call x1, Pallas kernels, body(): pl.pallas_call(functools.partial(kernel, Z, Y), out_shape=jax.ShapeDtypeS...  159 us
    unnamed x1, local copies, waits for them, and re-layouts  4.7 us

commit v1 on v0

--- a/solution.py
+++ b/solution.py
@@ -17,8 +17,8 @@
 
 
 def kernel(
-    Z, Y, q_ref, k_ref, v_ref, t_ref, w_ref, o_ref,
-    q_all, kv, t_all, t_smem, w_all, att, att_full, send, recv, local,
+    Z, Y, online, q_ref, k_ref, v_ref, t_ref, w_ref, o_ref,
+    q_all, kv, kv_left, kv_right, t_all, t_smem, w_all, att, att_full, m_ref, l_ref, acc_ref, send, recv, local,
 ):
     cell = 2 * Y
     hp = KVH // cell
@@ -91,6 +91,9 @@
         n = cell * nq
         return kv.at[:, pl.ds(origin * n, n)]
 
+    def own_blocks(which, idx):
+        return kv.at[which, pl.ds((idx if online else z * cell + idx) * nq, nq)]
+
     def z_copies(ids, src_of, dst_of, t):
         right = (has_right & (z - t >= 0), lambda: rcopy(ids[0], src_of(z - t), dst_of(z - t), g, s + cell))
         left = (has_left & (z + t <= Z - 1), lambda: rcopy(ids[1], src_of(z + t), dst_of(z + t), g, s - cell))
@@ -116,9 +119,9 @@
 
     loc = [
         pltpu.make_async_copy(k_ref.at[:, :, pl.ds(pl.multiple_of(i * kc, 128), kc)],
-                              kv.at[0, pl.ds(s * nq, nq)], local.at[0]),
+                              own_blocks(0, i), local.at[0]),
         pltpu.make_async_copy(v_ref.at[:, :, pl.ds(pl.multiple_of(i * kc, 128), kc)],
-                              kv.at[1, pl.ds(s * nq, nq)], local.at[1]),
+                              own_blocks(1, i), local.at[1]),
         pltpu.make_async_copy(q_ref.at[:, pl.ds(pl.multiple_of(i * qc, 128), qc)],
                               q_all.at[pl.ds(pl.multiple_of(i * tok, 128), tok), :], local.at[2]),
         pltpu.make_async_copy(t_ref, t_all.at[i], local.at[3]),
@@ -141,6 +144,13 @@
         return z_copies(wz_ids[t], same, same, t)
 
     def kz(t):
+        if online:
+            ids = kz_ids[t]
+            to_right = lambda: rcopy(ids[0], kv_left[t - 1] if t else kv, kv_left[t], g, s + cell)
+            to_left = lambda: rcopy(ids[1], kv_right[t - 1] if t else kv, kv_right[t], g, s - cell)
+            right = (has_right & (z - t >= 0), to_right)
+            left = (has_left & (z + t <= Z - 1), to_left)
+            return (right, left), ((z - 1 - t >= 0, to_right), (z + 1 + t <= Z - 1, to_left))
         return z_copies(kz_ids[t], layer_rows, layer_rows, t)
 
     for cond, make in wz(0)[0]:
@@ -153,10 +163,10 @@
 
             def make(n=n, p=p, which=which, ref=ref):
                 return rcopy(n, ref.at[:, :, pl.ds(pl.multiple_of(p * kc, 128), kc)],
-                             kv.at[which, pl.ds(s * nq, nq)], g, z * cell + p)
+                             own_blocks(which, i), g, z * cell + p)
 
             def landed(n=n, p=p, which=which):
-                at = kv.at[which, pl.ds((z * cell + p) * nq, nq)]
+                at = own_blocks(which, p)
                 return rcopy(n, at, at, g, z * cell + p)
 
             start(make)
@@ -231,8 +241,9 @@
         else:
             wait_recv_if(cond, make)
 
-    def relay_y():
-        while y_lands:
+    def relay_y(count=1 << 20):
+        while y_lands and count > 0:
+            count -= 1
             origin, cond, entry = y_lands.pop(0)
             maybe_wait(entry)
             x_lands.append((origin, cond, yi, w_send(
@@ -240,8 +251,9 @@
                 lambda origin=origin: wunit(origin, yi, 1 - xh), cond)))
             final.append(send_core(origin, yi, xh, y_cores, xh, cond))
 
-    def relay_x():
-        while x_lands:
+    def relay_x(count=1 << 20):
+        while x_lands and count > 0:
+            count -= 1
             origin, cond, idx, entry = x_lands.pop(0)
             maybe_wait(entry)
             there = cores if idx is i else y_cores
@@ -263,6 +275,87 @@
             for cond, make in kz(t + 1)[0]:
                 start_if(cond, make)
 
+    factor = HD ** -0.5 * LOG2E
+    n_seq = Z * cell
+    stride = n_seq // ENTRIES
+
+    def softmax_pass(keys, vals, rows, hh, pair, block, first, last):
+        cols = [pl.ds((hh * gh + pair * 2 + h) * HD, HD) for h in range(2)]
+        qq = jnp.concatenate([q_all[rows, cc] for cc in cols], 0)
+        sc = lax.dot_general(qq, keys, (((1,), (1,)), ((), ())), preferred_element_type=jnp.float32)
+        top = jnp.max(sc, axis=-1, keepdims=True)
+        kept = pl.ds(pl.multiple_of((block * gh + pair * 2) * QB, 2 * QB), 2 * QB)
+        if not first:
+            before = m_ref[kept, :1]
+            top = jnp.maximum(before, top)
+        wts = jnp.exp2((sc - top) * factor)
+        total = jnp.sum(wts, axis=-1, keepdims=True)
+        mixed = jnp.dot(wts.astype(jnp.bfloat16), vals, preferred_element_type=jnp.float32)
+        if not first:
+            shrink = jnp.exp2((before - top) * factor)
+            total = total + l_ref[kept, :1] * shrink
+            mixed = mixed + acc_ref[kept, :] * shrink
+        if last:
+            mixed = (mixed / total).astype(jnp.bfloat16)
+            for h in range(2):
+                att[rows, cols[h]] = mixed[h * QB:(h + 1) * QB]
+        else:
+            m_ref[kept, :] = jnp.broadcast_to(top, (2 * QB, HD))
+            l_ref[kept, :] = jnp.broadcast_to(total, (2 * QB, HD))
+            acc_ref[kept, :] = mixed
+
+    def attend(owner, parts, first, last):
+        def step(b, carry):
+            rows = pl.ds(pl.multiple_of(owner * tok + b * QB, QB), QB)
+            if parts is None:
+                picks = [(kv, t_smem[owner, b, e]) for e in range(ENTRIES)]
+            else:
+                base = z * cell + owner - lax.rem(b, 2) + n_seq
+                picks = []
+                for ref, layer in parts:
+                    for r in range(cell // stride):
+                        index = layer * cell + lax.rem(base, stride) + r * stride
+                        e = lax.div(lax.rem(index - base + 2 * n_seq, n_seq), stride)
+                        picks.append((ref, lax.rem(t_smem[owner, b, e], cell * nq)))
+            for hh in range(hp):
+                kcols = pl.ds(hh * HD, HD)
+                keys = jnp.concatenate([ref[0, n, :, kcols] for ref, n in picks], 0)
+                vals = jnp.concatenate([ref[1, n, :, kcols] for ref, n in picks], 0)
+                for pair in range(gh // 2):
+                    softmax_pass(keys, vals, rows, hh, pair, owner * nq + b, first, last)
+            return carry
+
+        lax.fori_loop(0, nq, step, 0)
+
+    def attend_all(parts, first):
+        def step(owner, carry):
+            attend(owner, parts, first, False)
+            return carry
+
+        lax.fori_loop(0, cell, step, 0)
+
+    def if_layer(layer):
+        return pl.when(z == layer)
+
+    def attend_last(owner):
+        if not online:
+            attend(owner, None, True, True)
+            return
+        for layer in range(Z):
+            t = max(layer, Z - 1 - layer) - 1
+            part = (kv_left[t], layer - 1 - t) if layer >= Z // 2 else (kv_right[t], layer + 1 + t)
+
+            @if_layer(layer)
+            def _(part=part):
+                attend(owner, [part], False, True)
+
+    def have_queries():
+        for make in q_in:
+            make().wait_recv()
+        tcp = pltpu.make_async_copy(t_all, t_smem, local.at[5])
+        tcp.start()
+        tcp.wait()
+
     w_step(0)
     for make in kv_in:
         make().wait_recv()
@@ -270,49 +363,48 @@
         cp.wait()
     for cond, make in kz(0)[0]:
         start_if(cond, make)
-    for t in range(1, Z - 1):
-        w_step(t)
-    k_step(0)
-    relay_y()
-    for t in range(1, Z - 1):
-        k_step(t)
-    relay_x()
-
-    for make in q_in:
-        make().wait_recv()
-    tcp = pltpu.make_async_copy(t_all, t_smem, local.at[5])
-    tcp.start()
-    tcp.wait()
-
-    factor = HD ** -0.5 * LOG2E
-
-    def attend(owner):
-        def block(b, carry):
-            rows = pl.ds(pl.multiple_of(owner * tok + b * QB, QB), QB)
-            ids = [t_smem[owner, b, e] for e in range(ENTRIES)]
-            for hh in range(hp):
-                kcols = pl.ds(hh * HD, HD)
-                keys = jnp.concatenate([kv[0, n, :, kcols] for n in ids], 0)
-                vals = jnp.concatenate([kv[1, n, :, kcols] for n in ids], 0)
-                for pair in range(gh // 2):
-                    cols = [pl.ds((hh * gh + pair * 2 + h) * HD, HD) for h in range(2)]
-                    qq = jnp.concatenate([q_all[rows, cc] for cc in cols], 0)
-                    sc = lax.dot_general(qq, keys, (((1,), (1,)), ((), ())),
-                                         preferred_element_type=jnp.float32)
-                    top = jnp.max(sc, axis=-1, keepdims=True)
-                    wts = jnp.exp2((sc - top) * factor)
-                    total = jnp.sum(wts, axis=-1, keepdims=True)
-                    mixed = jnp.dot(wts.astype(jnp.bfloat16), vals, preferred_element_type=jnp.float32)
-                    mixed = (mixed / total).astype(jnp.bfloat16)
-                    for h in range(2):
-                        att[rows, cols[h]] = mixed[h * QB:(h + 1) * QB]
-            return carry
-
-        lax.fori_loop(0, nq, block, 0)
+    if online:
+        w_step(1)
+        relay_y(1)
+        w_step(2)
+        k_step(0)
+        relay_y(2)
+        have_queries()
+        for layer in range(Z):
+            parts = [(kv, layer)]
+            if layer > 0:
+                parts.append((kv_left[0], layer - 1))
+            if layer < Z - 1:
+                parts.append((kv_right[0], layer + 1))
+
+            @if_layer(layer)
+            def _(parts=parts):
+                attend_all(parts, True)
+
+        relay_y()
+        k_step(1)
+        relay_x(4)
+        for layer, part in ((0, (kv_right[1], 2)), (Z - 1, (kv_left[1], Z - 3))):
+
+            @if_layer(layer)
+            def _(part=part):
+                attend_all([part], False)
+
+        relay_x(5)
+        k_step(2)
+    else:
+        for t in range(1, Z - 1):
+            w_step(t)
+        k_step(0)
+        relay_y()
+        for t in range(1, Z - 1):
+            k_step(t)
+        relay_x()
+        have_queries()
 
     att_in = []
     for p in partners:
-        attend(p)
+        attend_last(p)
         n = new_id()
 
         def make(n=n, p=p):
@@ -325,7 +417,8 @@
 
         start(make)
         att_in.append(landed)
-    attend(i)
+    relay_x()
+    attend_last(i)
     own = pltpu.make_async_copy(att.at[pl.ds(pl.multiple_of(i * tok, 128), tok), :],
                                 att_full.at[:, pl.ds(pl.multiple_of(i * qc, 128), qc)], local.at[6])
     own.start()
@@ -357,24 +450,32 @@
     cell = 2 * Y
     hp = KVH // cell
     D = out_weight.shape[1]
-    table = jnp.pad(block_table, ((0, 8 - block_table.shape[0]), (0, 128 - ENTRIES)))
+    table = block_table
+    online = Z == 4 and cell % (Z * cell // ENTRIES) == 0
+    state = (cell * tok * H // KVH, HD) if online else (8, HD)
     blocks = (tok // QB, QB, KVH * HD)
+    part = (2, cell * tok // QB, QB, hp * HD)
     steps = Z - 1
     n_sems = steps * 4 + (cell - 1) * 5 + 8 + steps * 2 * 9
     flops = 2 * tok * width * D + 4 * tok * H * ENTRIES * QB * HD
     return pl.pallas_call(
-        functools.partial(kernel, Z, Y),
+        functools.partial(kernel, Z, Y, online),
         out_shape=jax.ShapeDtypeStruct((tok, D), jnp.bfloat16),
         in_specs=[pl.BlockSpec(memory_space=pl.ANY)] * 5,
         out_specs=pl.BlockSpec(memory_space=pltpu.VMEM),
         scratch_shapes=[
             pltpu.VMEM((cell * tok, width // cell), jnp.bfloat16),
-            pltpu.VMEM((2, Z * cell * tok // QB, QB, hp * HD), jnp.bfloat16),
-            pltpu.VMEM((cell, 8, 128), jnp.int32),
-            pltpu.SMEM((cell, 8, 128), jnp.int32),
+            pltpu.VMEM(part if online else (2, Z * cell * tok // QB, QB, hp * HD), jnp.bfloat16),
+            [pltpu.VMEM(part, jnp.bfloat16)] * (steps if online else 0),
+            [pltpu.VMEM(part, jnp.bfloat16)] * (steps if online else 0),
+            pltpu.VMEM((cell,) + table.shape, jnp.int32),
+            pltpu.SMEM((cell,) + table.shape, jnp.int32),
             pltpu.VMEM((out_weight.shape[0] * Z * cell, D), jnp.bfloat16),
             pltpu.VMEM((cell * tok, width // cell), jnp.bfloat16),
             pltpu.VMEM((tok, width), jnp.bfloat16),
+            pltpu.VMEM(state, jnp.float32),
+            pltpu.VMEM(state, jnp.float32),
+            pltpu.VMEM(state, jnp.float32),
             pltpu.SemaphoreType.DMA((n_sems,)),
             pltpu.SemaphoreType.DMA((n_sems,)),
             pltpu.SemaphoreType.DMA((7,)),

time: 166 us -> 159 us (0.958)
  Pallas kernels: 159 us -> 154 us
    pallas_call x1, Pallas kernels: 159 us -> 154 us  [body(): pl.pallas_call(functools.partial(kernel, Z, Y, online), out_shape=jax.Sha...]
where the time goes in v1:
time: 159 us
  Pallas kernels  154 us (97%)
  local copies, waits for them, and re-layouts  4.7 us (3%)
    pallas_call x1, Pallas kernels, body(): pl.pallas_call(functools.partial(kernel, Z, Y, online), out_shape=jax.Sha...  154 us
    unnamed x1, local copies, waits for them, and re-layouts  4.7 us

profile of v1, /device:TPU:0, one launch (start us, length us, event | category | flops | bytes accessed | tf_op | source)
XLA Modules:
  0.0 158.7 jit_solution(4094270302744838916)
XLA Ops:
  0.0 154.0 %shard_map.55 = bf16[512,4096]{1,0:T(8,128)(2,1)} custom-call(bf16[512,2048]{1,0:T(8,128)(2,1)} %q_ref.1, bf16[4,128,512]{2,1,0:T(8,128)(2,1)} %bitcast.2, bf16[4,128,512]{2,1,0:T(8,128)(2,1)} %bitcast.3, s32[4,8]{1,0:T(4,128)} %t_ref.1, bf16[128,4096]{1,0:T(8,128)(2,1)} %w_ref.1), custom_call_target="tpu_custom_call" | custom-call | flops 12884901888 | bytes 67108864 | tf_op jit(solution)/shard_map/pallas_call | solution.py:461
  154.0 4.7 %copy.7 = bf16[512,4096]{1,0:T(8,128)(2,1)} copy(bf16[512,4096]{1,0:T(8,128)(2,1)} %shard_map.55) | data formatting | bytes 8388608

commit v2 on v1

--- a/solution.py
+++ b/solution.py
@@ -17,8 +17,8 @@
 
 
 def kernel(
-    Z, Y, online, q_ref, k_ref, v_ref, t_ref, w_ref, o_ref,
-    q_all, kv, kv_left, kv_right, t_all, t_smem, w_all, att, att_full, m_ref, l_ref, acc_ref, send, recv, local,
+    Z, Y, online, q_ref, k_ref, v_ref, t_ref, w_ref, att_full, w_all,
+    q_all, kv, kv_left, kv_right, t_all, t_smem, att, m_ref, l_ref, acc_ref, send, recv, local,
 ):
     cell = 2 * Y
     hp = KVH // cell
@@ -156,7 +156,7 @@
     for cond, make in wz(0)[0]:
         start_if(cond, make)
 
-    kv_in, q_in, t_in = [], [], []
+    kv_in = []
     for p in partners:
         for which, ref in ((0, k_ref), (1, v_ref)):
             n = new_id()
@@ -189,38 +189,40 @@
         return w_send(lambda: wunit(origin, idx, xx), lambda: wunit(origin, idx, xx), g, core_dev,
                       lambda: wunit(origin, idx_there, xx_there), cond)
 
-    final = []
-    n_own = new_id()
-    own_core = lambda: rcopy(n_own, w_ref, wpair(z, i), g, core_dev)
-    start(own_core)
-    final.append((None, lambda: rcopy(n_own, wpair(z, cores), wpair(z, cores), g, core_dev)))
-    y_lands = []
-    if Y == 2:
-        y_lands.append((z, None, w_send(lambda: w_src0(z), lambda: wunit(z, i, xh), g, y_dev,
-                                        lambda: wunit(z, yi, xh))))
-    for p in partners:
-        n = new_id()
-
-        def make(n=n, p=p):
-            return rcopy(n, q_ref.at[:, pl.ds(pl.multiple_of(p * qc, 128), qc)],
-                         q_all.at[pl.ds(pl.multiple_of(i * tok, 128), tok), :], g, z * cell + p)
-
-        def landed(n=n, p=p):
-            at = q_all.at[pl.ds(pl.multiple_of(p * tok, 128), tok), :]
-            return rcopy(n, at, at, g, z * cell + p)
-
-        start(make)
-        q_in.append(landed)
-        m = new_id()
-
-        def make_t(m=m, p=p):
-            return rcopy(m, t_ref, t_all.at[i], g, z * cell + p)
-
-        def landed_t(m=m, p=p):
-            return rcopy(m, t_all.at[p], t_all.at[p], g, z * cell + p)
-
-        start(make_t)
-        q_in.append(landed_t)
+    final, y_lands, q_in = [], [], []
+
+    def send_rest():
+        n_own = new_id()
+        own_core = lambda: rcopy(n_own, w_ref, wpair(z, i), g, core_dev)
+        start(own_core)
+        final.append((None, lambda: rcopy(n_own, wpair(z, cores), wpair(z, cores), g, core_dev)))
+        if Y == 2:
+            y_lands.append((z, None, w_send(lambda: w_src0(z), lambda: wunit(z, i, xh), g, y_dev,
+                                            lambda: wunit(z, yi, xh))))
+        for p in partners:
+            n = new_id()
+
+            def make(n=n, p=p):
+                return rcopy(n, q_ref.at[:, pl.ds(pl.multiple_of(p * qc, 128), qc)],
+                             q_all.at[pl.ds(pl.multiple_of(i * tok, 128), tok), :], g, z * cell + p)
+
+            def landed(n=n, p=p):
+                at = q_all.at[pl.ds(pl.multiple_of(p * tok, 128), tok), :]
+                return rcopy(n, at, at, g, z * cell + p)
+
+            start(make)
+            q_in.append(landed)
+            m = new_id()
+
+            def make_t(m=m, p=p):
+                return rcopy(m, t_ref, t_all.at[i], g, z * cell + p)
+
+            def landed_t(m=m, p=p):
+                return rcopy(m, t_all.at[p], t_all.at[p], g, z * cell + p)
+
+            start(make_t)
+            q_in.append(landed_t)
+
 
     x_lands = []
 
@@ -356,13 +358,16 @@
         tcp.start()
         tcp.wait()
 
-    w_step(0)
+    for cp in loc[:2]:
+        cp.wait()
     for make in kv_in:
         make().wait_recv()
-    for cp in loc:
-        cp.wait()
     for cond, make in kz(0)[0]:
         start_if(cond, make)
+    send_rest()
+    w_step(0)
+    for cp in loc[2:]:
+        cp.wait()
     if online:
         w_step(1)
         relay_y(1)
@@ -428,14 +433,6 @@
     for entry in final:
         maybe_wait(entry)
 
-    tile = 512
-    def project(j, carry):
-        cols = pl.ds(pl.multiple_of(j * tile, tile), tile)
-        o_ref[:, cols] = jnp.dot(att_full[...], w_all[:, cols],
-                                 preferred_element_type=jnp.float32).astype(jnp.bfloat16)
-        return carry
-
-    lax.fori_loop(0, o_ref.shape[1] // tile, project, 0)
     for cond, make in pending:
         if cond is None:
             make().wait_send()
@@ -443,6 +440,10 @@
             @pl.when(cond)
             def _(make=make):
                 make().wait_send()
+
+
+def project(a_ref, w_ref, o_ref):
+    o_ref[...] = jnp.dot(a_ref[...], w_ref[...], preferred_element_type=jnp.float32).astype(o_ref.dtype)
 
 
 def body(Z, Y, queries, keys, values, block_table, out_weight):
@@ -457,12 +458,16 @@
     part = (2, cell * tok // QB, QB, hp * HD)
     steps = Z - 1
     n_sems = steps * 4 + (cell - 1) * 5 + 8 + steps * 2 * 9
-    flops = 2 * tok * width * D + 4 * tok * H * ENTRIES * QB * HD
-    return pl.pallas_call(
+    flops = 4 * tok * H * ENTRIES * QB * HD
+    depth = out_weight.shape[0] * Z * cell
+    attended, weight = pl.pallas_call(
         functools.partial(kernel, Z, Y, online),
-        out_shape=jax.ShapeDtypeStruct((tok, D), jnp.bfloat16),
+        out_shape=(
+            jax.ShapeDtypeStruct((tok, width), jnp.bfloat16),
+            jax.ShapeDtypeStruct((depth, D), jnp.bfloat16),
+        ),
         in_specs=[pl.BlockSpec(memory_space=pl.ANY)] * 5,
-        out_specs=pl.BlockSpec(memory_space=pltpu.VMEM),
+        out_specs=(pl.BlockSpec(memory_space=pl.ANY), pl.BlockSpec(memory_space=pl.ANY)),
         scratch_shapes=[
             pltpu.VMEM((cell * tok, width // cell), jnp.bfloat16),
             pltpu.VMEM(part if online else (2, Z * cell * tok // QB, QB, hp * HD), jnp.bfloat16),
@@ -470,9 +475,7 @@
             [pltpu.VMEM(part, jnp.bfloat16)] * (steps if online else 0),
             pltpu.VMEM((cell,) + table.shape, jnp.int32),
             pltpu.SMEM((cell,) + table.shape, jnp.int32),
-            pltpu.VMEM((out_weight.shape[0] * Z * cell, D), jnp.bfloat16),
             pltpu.VMEM((cell * tok, width // cell), jnp.bfloat16),
-            pltpu.VMEM((tok, width), jnp.bfloat16),
             pltpu.VMEM(state, jnp.float32),
             pltpu.VMEM(state, jnp.float32),
             pltpu.VMEM(state, jnp.float32),
@@ -485,6 +488,20 @@
         ),
         cost_estimate=pl.CostEstimate(flops=flops, bytes_accessed=64 * 1024 * 1024, transcendentals=0),
     )(queries, keys.reshape(blocks), values.reshape(blocks), table, out_weight)
+    tile = 512
+    return pl.pallas_call(
+        project,
+        grid=(D // tile,),
+        out_shape=jax.ShapeDtypeStruct((tok, D), jnp.bfloat16),
+        in_specs=[
+            pl.BlockSpec((tok, depth), lambda j: (0, 0)),
+            pl.BlockSpec((depth, tile), lambda j: (0, j)),
+        ],
+        out_specs=pl.BlockSpec((tok, tile), lambda j: (0, j)),
+        compiler_params=pltpu.CompilerParams(vmem_limit_bytes=40 * 1024 * 1024),
+        cost_estimate=pl.CostEstimate(
+            flops=2 * tok * depth * D, bytes_accessed=2 * (tok * depth + depth * D + tok * D), transcendentals=0),
+    )(attended, weight)
 
 
 def solution(mesh):

time: 159 us -> 157 us (0.987)
  local copies, waits for them, and re-layouts: 4.7 us -> 1.58 us
    unnamed x1 -> x2, local copies, waits for them, and re-layouts: 4.7 us -> 1.58 us
    pallas_call x1 -> x2, Pallas kernels: 154 us -> 155 us  [the longest x1 141 us: body(): pl.pallas_call(functools.partial(kernel, Z, Y, online), out_shape=(jax.Sh...]
where the time goes in v2:
time: 157 us
  Pallas kernels  155 us (99%)
  local copies, waits for them, and re-layouts  1.58 us (1%)
    pallas_call x1, Pallas kernels, body(): pl.pallas_call(functools.partial(kernel, Z, Y, online), out_shape=(jax.Sh...  141 us
    pallas_call x1, Pallas kernels, body(): pl.pallas_call(project, grid=(D // tile,), out_shape=jax.ShapeDtypeStruct...  14.3 us

profile of v2, /device:TPU:0, one launch (start us, length us, event | category | flops | bytes accessed | tf_op | source)
XLA Modules:
  0.0 156.8 jit_solution(4531443183265521658)
XLA Ops:
  0.0 140.9 %shard_map.55 = (bf16[512,2048]{1,0:T(8,128)(2,1)}, bf16[2048,4096]{1,0:T(8,128)(2,1)}) custom-call(bf16[512,2048]{1,0:T(8,128)(2,1)} %q_ref.1, bf16[4,128,512]{2,1,0:T(8,128)(2,1)} %bitcast.2, bf16[4,128,512]{2,1,0:T(8,128)(2,1)} %bitcast.3, s32[4,8]{1,0:T(4,128)} %t_ref.1, bf16[128,4096]{1,0:T(8,128)(2,1)} %w_ref.1), custom_call_target="tpu_custom_call" | custom-call | flops 4294967296 | bytes 67108864 | tf_op jit(solution)/shard_map/pallas_call | solution.py:463
  140.9 0.0 copy-start
  140.9 1.6 %copy-done = bf16[512,2048]{1,0:T(8,128)(2,1)S(1)} copy-done((bf16[512,2048]{1,0:T(8,128)(2,1)S(1)}, bf16[512,2048]{1,0:T(8,128)(2,1)}, u32[]{:S(2)}) %copy-start) | copy-done | bytes 2097176
  142.5 14.3 %shard_map.56 = bf16[512,4096]{1,0:T(8,128)(2,1)} custom-call(bf16[512,2048]{1,0:T(8,128)(2,1)S(1)} %copy-done, bf16[2048,4096]{1,0:T(8,128)(2,1)} %get-tuple-element.8.w_ref), custom_call_target="tpu_custom_call" | custom-call | flops 8589934592 | bytes 23068672 | tf_op jit(solution)/shard_map/pallas_call | solution.py:492
Async XLA Ops:
  140.9 1.6 %copy-start = (bf16[512,2048]{1,0:T(8,128)(2,1)S(1)}, bf16[512,2048]{1,0:T(8,128)(2,1)}, u32[]{:S(2)}) copy-start(bf16[512,2048]{1,0:T(8,128)(2,1)} %get-tuple-element.7.a_ref) | copy-start | bytes 6291460

commit v3 on v2

--- a/solution.py
+++ b/solution.py
@@ -281,30 +281,30 @@
     n_seq = Z * cell
     stride = n_seq // ENTRIES
 
-    def softmax_pass(keys, vals, rows, hh, pair, block, first, last):
-        cols = [pl.ds((hh * gh + pair * 2 + h) * HD, HD) for h in range(2)]
+    def softmax_pass(keys, vals, rows, hh, block, first, last):
+        cols = [pl.ds((hh * gh + h) * HD, HD) for h in range(gh)]
         qq = jnp.concatenate([q_all[rows, cc] for cc in cols], 0)
-        sc = lax.dot_general(qq, keys, (((1,), (1,)), ((), ())), preferred_element_type=jnp.float32)
-        top = jnp.max(sc, axis=-1, keepdims=True)
-        kept = pl.ds(pl.multiple_of((block * gh + pair * 2) * QB, 2 * QB), 2 * QB)
+        sc = lax.dot_general(keys, qq, (((1,), (1,)), ((), ())), preferred_element_type=jnp.float32)
+        top = jnp.max(sc, axis=0, keepdims=True)
         if not first:
-            before = m_ref[kept, :1]
+            before = m_ref[block]
             top = jnp.maximum(before, top)
         wts = jnp.exp2((sc - top) * factor)
-        total = jnp.sum(wts, axis=-1, keepdims=True)
-        mixed = jnp.dot(wts.astype(jnp.bfloat16), vals, preferred_element_type=jnp.float32)
+        total = jnp.sum(wts, axis=0, keepdims=True)
+        mixed = lax.dot_general(vals, wts.astype(jnp.bfloat16), (((0,), (0,)), ((), ())),
+                                preferred_element_type=jnp.float32)
         if not first:
             shrink = jnp.exp2((before - top) * factor)
-            total = total + l_ref[kept, :1] * shrink
-            mixed = mixed + acc_ref[kept, :] * shrink
+            total = total + l_ref[block] * shrink
+            mixed = mixed + acc_ref[block] * shrink
         if last:
-            mixed = (mixed / total).astype(jnp.bfloat16)
-            for h in range(2):
-                att[rows, cols[h]] = mixed[h * QB:(h + 1) * QB]
+            mixed = mixed / total
+            for h in range(gh):
+                att[rows, cols[h]] = mixed[:, h * QB:(h + 1) * QB].T.astype(jnp.bfloat16)
         else:
-            m_ref[kept, :] = jnp.broadcast_to(top, (2 * QB, HD))
-            l_ref[kept, :] = jnp.broadcast_to(total, (2 * QB, HD))
-            acc_ref[kept, :] = mixed
+            m_ref[block] = top
+            l_ref[block] = total
+            acc_ref[block] = mixed
 
     def attend(owner, parts, first, last):
         def step(b, carry):
@@ -323,8 +323,7 @@
                 kcols = pl.ds(hh * HD, HD)
                 keys = jnp.concatenate([ref[0, n, :, kcols] for ref, n in picks], 0)
                 vals = jnp.concatenate([ref[1, n, :, kcols] for ref, n in picks], 0)
-                for pair in range(gh // 2):
-                    softmax_pass(keys, vals, rows, hh, pair, owner * nq + b, first, last)
+                softmax_pass(keys, vals, rows, hh, owner * nq + b, first, last)
             return carry
 
         lax.fori_loop(0, nq, step, 0)
@@ -344,12 +343,26 @@
             attend(owner, None, True, True)
             return
         for layer in range(Z):
-            t = max(layer, Z - 1 - layer) - 1
-            part = (kv_left[t], layer - 1 - t) if layer >= Z // 2 else (kv_right[t], layer + 1 + t)
+            near = first_parts(layer)
+            parts = [part for part in brought(layer) if part[1] not in [p[1] for p in near]]
+            if layer in (0, Z - 1):
+                parts = parts[-1:]
 
             @if_layer(layer)
-            def _(part=part):
-                attend(owner, [part], False, True)
+            def _(parts=parts):
+                attend(owner, parts, False, True)
+
+    def brought(layer):
+        parts = []
+        for t in range(Z - 1):
+            if layer - 1 - t >= 0:
+                parts.append((kv_left[t], layer - 1 - t))
+            if layer + 1 + t < Z:
+                parts.append((kv_right[t], layer + 1 + t))
+        return parts
+
+    def first_parts(layer):
+        return [(kv, layer), brought(layer)[0]]
 
     def have_queries():
         for make in q_in:
@@ -376,26 +389,22 @@
         relay_y(2)
         have_queries()
         for layer in range(Z):
-            parts = [(kv, layer)]
-            if layer > 0:
-                parts.append((kv_left[0], layer - 1))
-            if layer < Z - 1:
-                parts.append((kv_right[0], layer + 1))
+            parts = first_parts(layer)
 
             @if_layer(layer)
             def _(parts=parts):
                 attend_all(parts, True)
 
+        k_step(1)
         relay_y()
-        k_step(1)
-        relay_x(4)
+        relay_x(5)
         for layer, part in ((0, (kv_right[1], 2)), (Z - 1, (kv_left[1], Z - 3))):
 
             @if_layer(layer)
             def _(part=part):
                 attend_all([part], False)
 
-        relay_x(5)
+        relay_x(4)
         k_step(2)
     else:
         for t in range(1, Z - 1):
@@ -453,7 +462,8 @@
     D = out_weight.shape[1]
     table = block_table
     online = Z == 4 and cell % (Z * cell // ENTRIES) == 0
-    state = (cell * tok * H // KVH, HD) if online else (8, HD)
+    blocks_here = cell * tok // QB if online else 1
+    rows = H // KVH * QB
     blocks = (tok // QB, QB, KVH * HD)
     part = (2, cell * tok // QB, QB, hp * HD)
     steps = Z - 1
@@ -476,9 +486,9 @@
             pltpu.VMEM((cell,) + table.shape, jnp.int32),
             pltpu.SMEM((cell,) + table.shape, jnp.int32),
             pltpu.VMEM((cell * tok, width // cell), jnp.bfloat16),
-            pltpu.VMEM(state, jnp.float32),
-            pltpu.VMEM(state, jnp.float32),
-            pltpu.VMEM(state, jnp.float32),
+            pltpu.VMEM((blocks_here, 1, rows), jnp.float32),
+            pltpu.VMEM((blocks_here, 1, rows), jnp.float32),
+            pltpu.VMEM((blocks_here, HD, rows), jnp.float32),
             pltpu.SemaphoreType.DMA((n_sems,)),
             pltpu.SemaphoreType.DMA((n_sems,)),
             pltpu.SemaphoreType.DMA((7,)),
@@ -498,7 +508,7 @@
             pl.BlockSpec((depth, tile), lambda j: (0, j)),
         ],
         out_specs=pl.BlockSpec((tok, tile), lambda j: (0, j)),
-        compiler_params=pltpu.CompilerParams(vmem_limit_bytes=40 * 1024 * 1024),
+        compiler_params=pltpu.CompilerParams(vmem_limit_bytes=60 * 1024 * 1024),
         cost_estimate=pl.CostEstimate(
             flops=2 * tok * depth * D, bytes_accessed=2 * (tok * depth + depth * D + tok * D), transcendentals=0),
     )(attended, weight)

time: 157 us -> 151 us (0.962)
  Pallas kernels: 155 us -> 151 us
  local copies, waits for them, and re-layouts: 1.58 us -> 0 us
    pallas_call x1, Pallas kernels: 141 us -> 136 us  [body(): pl.pallas_call(functools.partial(kernel, Z, Y, online), out_shape=(jax.Sh...]
    unnamed x2 -> x0, local copies, waits for them, and re-layouts: 1.58 us -> none
where the time goes in v3:
time: 151 us
  Pallas kernels  151 us (100%)
    pallas_call x1, Pallas kernels, body(): pl.pallas_call(functools.partial(kernel, Z, Y, online), out_shape=(jax.Sh...  136 us
    pallas_call x1, Pallas kernels, body(): pl.pallas_call(project, grid=(D // tile,), out_shape=jax.ShapeDtypeStruct...  15 us

profile of v3, /device:TPU:0, one launch (start us, length us, event | category | flops | bytes accessed | tf_op | source)
XLA Modules:
  0.0 150.7 jit_solution(13841087180225826912)
XLA Ops:
  0.0 135.7 %shard_map.55 = (bf16[512,2048]{1,0:T(8,128)(2,1)}, bf16[2048,4096]{1,0:T(8,128)(2,1)}) custom-call(bf16[512,2048]{1,0:T(8,128)(2,1)} %q_ref.1, bf16[4,128,512]{2,1,0:T(8,128)(2,1)} %bitcast.2, bf16[4,128,512]{2,1,0:T(8,128)(2,1)} %bitcast.3, s32[4,8]{1,0:T(4,128)} %t_ref.1, bf16[128,4096]{1,0:T(8,128)(2,1)} %w_ref.1), custom_call_target="tpu_custom_call" | custom-call | flops 4294967296 | bytes 67108864 | tf_op jit(solution)/shard_map/pallas_call | solution.py:473
  135.7 15.0 %shard_map.56 = bf16[512,4096]{1,0:T(8,128)(2,1)} custom-call(bf16[512,2048]{1,0:T(8,128)(2,1)} %get-tuple-element.7.a_ref, bf16[2048,4096]{1,0:T(8,128)(2,1)} %get-tuple-element.8.w_ref), custom_call_target="tpu_custom_call" | custom-call | flops 8589934592 | bytes 23068672 | tf_op jit(solution)/shard_map/pallas_call | solution.py:502

commit v4 on v3

--- a/solution.py
+++ b/solution.py
@@ -191,7 +191,7 @@
 
     final, y_lands, q_in = [], [], []
 
-    def send_rest():
+    def send_own_weight():
         n_own = new_id()
         own_core = lambda: rcopy(n_own, w_ref, wpair(z, i), g, core_dev)
         start(own_core)
@@ -199,6 +199,8 @@
         if Y == 2:
             y_lands.append((z, None, w_send(lambda: w_src0(z), lambda: wunit(z, i, xh), g, y_dev,
                                             lambda: wunit(z, yi, xh))))
+
+    def send_queries():
         for p in partners:
             n = new_id()
 
@@ -343,10 +345,7 @@
             attend(owner, None, True, True)
             return
         for layer in range(Z):
-            near = first_parts(layer)
-            parts = [part for part in brought(layer) if part[1] not in [p[1] for p in near]]
-            if layer in (0, Z - 1):
-                parts = parts[-1:]
+            parts = brought(layer)[-1:]
 
             @if_layer(layer)
             def _(parts=parts):
@@ -361,9 +360,6 @@
                 parts.append((kv_right[t], layer + 1 + t))
         return parts
 
-    def first_parts(layer):
-        return [(kv, layer), brought(layer)[0]]
-
     def have_queries():
         for make in q_in:
             make().wait_recv()
@@ -371,42 +367,40 @@
         tcp.start()
         tcp.wait()
 
-    for cp in loc[:2]:
-        cp.wait()
-    for make in kv_in:
-        make().wait_recv()
-    for cond, make in kz(0)[0]:
-        start_if(cond, make)
-    send_rest()
+    def start_keys():
+        for cp in loc:
+            cp.wait()
+        for make in kv_in:
+            make().wait_recv()
+        for cond, make in kz(0)[0]:
+            start_if(cond, make)
+
+    send_own_weight()
     w_step(0)
-    for cp in loc[2:]:
-        cp.wait()
     if online:
         w_step(1)
-        relay_y(1)
+        start_keys()
+        relay_y(3)
         w_step(2)
+        relay_y(2)
         k_step(0)
-        relay_y(2)
+        relay_y()
+        send_queries()
+        relay_x(4)
+        k_step(1)
         have_queries()
         for layer in range(Z):
-            parts = first_parts(layer)
+            parts = [(kv, layer)] + brought(layer)[:-1]
 
             @if_layer(layer)
             def _(parts=parts):
                 attend_all(parts, True)
 
-        k_step(1)
-        relay_y()
-        relay_x(5)
-        for layer, part in ((0, (kv_right[1], 2)), (Z - 1, (kv_left[1], Z - 3))):
-
-            @if_layer(layer)
-            def _(part=part):
-                attend_all([part], False)
-
-        relay_x(4)
+        relay_x()
         k_step(2)
     else:
+        start_keys()
+        send_queries()
         for t in range(1, Z - 1):
             w_step(t)
         k_step(0)

time: 151 us -> 152 us (level)
  no operation moved by 1% of the time
where the time goes in v4:
time: 152 us
  Pallas kernels  152 us (100%)
    pallas_call x1, Pallas kernels, body(): pl.pallas_call(functools.partial(kernel, Z, Y, online), out_shape=(jax.Sh...  137 us
    pallas_call x1, Pallas kernels, body(): pl.pallas_call(project, grid=(D // tile,), out_shape=jax.ShapeDtypeStruct...  15 us

profile of v4, /device:TPU:0, one launch (start us, length us, event | category | flops | bytes accessed | tf_op | source)
XLA Modules:
  0.0 151.7 jit_solution(6920855972953124994)
XLA Ops:
  0.0 136.7 %shard_map.55 = (bf16[512,2048]{1,0:T(8,128)(2,1)}, bf16[2048,4096]{1,0:T(8,128)(2,1)}) custom-call(bf16[512,2048]{1,0:T(8,128)(2,1)} %q_ref.1, bf16[4,128,512]{2,1,0:T(8,128)(2,1)} %bitcast.2, bf16[4,128,512]{2,1,0:T(8,128)(2,1)} %bitcast.3, s32[4,8]{1,0:T(4,128)} %t_ref.1, bf16[128,4096]{1,0:T(8,128)(2,1)} %w_ref.1), custom_call_target="tpu_custom_call" | custom-call | flops 4294967296 | bytes 67108864 | tf_op jit(solution)/shard_map/pallas_call | solution.py:467
  136.7 15.0 %shard_map.56 = bf16[512,4096]{1,0:T(8,128)(2,1)} custom-call(bf16[512,2048]{1,0:T(8,128)(2,1)} %get-tuple-element.7.a_ref, bf16[2048,4096]{1,0:T(8,128)(2,1)} %get-tuple-element.8.w_ref), custom_call_target="tpu_custom_call" | custom-call | flops 8589934592 | bytes 23068672 | tf_op jit(solution)/shard_map/pallas_call | solution.py:496

commit v5 on v4

--- a/solution.py
+++ b/solution.py
@@ -87,9 +87,9 @@
         start = (origin * cell + idx) * wrows
         return w_all.at[pl.ds(pl.multiple_of(start, 16), wrows), :]
 
-    def layer_rows(origin):
+    def layer_rows(origin, a):
         n = cell * nq
-        return kv.at[:, pl.ds(origin * n, n)]
+        return kv.at[a, pl.ds(origin * n, n)]
 
     def own_blocks(which, idx):
         return kv.at[which, pl.ds((idx if online else z * cell + idx) * nq, nq)]
@@ -134,7 +134,7 @@
         return w_ref.at[pl.ds(pl.multiple_of(xh * half, 16), half), :]
 
     wz_ids = [(new_id(), new_id()) for _ in range(Z - 1)]
-    kz_ids = [(new_id(), new_id()) for _ in range(Z - 1)]
+    kz_ids = [[(new_id(), new_id()) for _ in range(2)] for _ in range(Z - 1)]
 
     def wz(t):
         if t == 0:
@@ -143,15 +143,17 @@
         same = lambda origin: wunit(origin, i, xh)
         return z_copies(wz_ids[t], same, same, t)
 
-    def kz(t):
+    def kz(t, a):
         if online:
-            ids = kz_ids[t]
-            to_right = lambda: rcopy(ids[0], kv_left[t - 1] if t else kv, kv_left[t], g, s + cell)
-            to_left = lambda: rcopy(ids[1], kv_right[t - 1] if t else kv, kv_right[t], g, s - cell)
+            ids = kz_ids[t][a]
+            left_at = lambda n: kv_left[n].at[a] if n >= 0 else kv.at[a]
+            right_at = lambda n: kv_right[n].at[a] if n >= 0 else kv.at[a]
+            to_right = lambda: rcopy(ids[0], left_at(t - 1), left_at(t), g, s + cell)
+            to_left = lambda: rcopy(ids[1], right_at(t - 1), right_at(t), g, s - cell)
             right = (has_right & (z - t >= 0), to_right)
             left = (has_left & (z + t <= Z - 1), to_left)
             return (right, left), ((z - 1 - t >= 0, to_right), (z + 1 + t <= Z - 1, to_left))
-        return z_copies(kz_ids[t], layer_rows, layer_rows, t)
+        return z_copies(kz_ids[t][a], lambda o: layer_rows(o, a), lambda o: layer_rows(o, a), t)
 
     for cond, make in wz(0)[0]:
         start_if(cond, make)
@@ -273,11 +275,12 @@
         spread(z + 1 + t, z + 1 + t <= Z - 1)
 
     def k_step(t):
-        for cond, make in kz(t)[1]:
-            wait_recv_if(cond, make)
-        if t + 1 < Z - 1:
-            for cond, make in kz(t + 1)[0]:
-                start_if(cond, make)
+        for a in (0, 1):
+            for cond, make in kz(t, a)[1]:
+                wait_recv_if(cond, make)
+            if t + 1 < Z - 1:
+                for cond, make in kz(t + 1, a)[0]:
+                    start_if(cond, make)
 
     factor = HD ** -0.5 * LOG2E
     n_seq = Z * cell
@@ -372,8 +375,9 @@
             cp.wait()
         for make in kv_in:
             make().wait_recv()
-        for cond, make in kz(0)[0]:
-            start_if(cond, make)
+        for a in (0, 1):
+            for cond, make in kz(0, a)[0]:
+                start_if(cond, make)
 
     send_own_weight()
     w_step(0)
@@ -461,7 +465,7 @@
     blocks = (tok // QB, QB, KVH * HD)
     part = (2, cell * tok // QB, QB, hp * HD)
     steps = Z - 1
-    n_sems = steps * 4 + (cell - 1) * 5 + 8 + steps * 2 * 9
+    n_sems = steps * 6 + (cell - 1) * 5 + 8 + steps * 2 * 9
     flops = 4 * tok * H * ENTRIES * QB * HD
     depth = out_weight.shape[0] * Z * cell
     attended, weight = pl.pallas_call(

time: 152 us -> 152 us (level)
  no operation moved by 1% of the time
where the time goes in v5:
time: 152 us
  Pallas kernels  152 us (100%)
    pallas_call x1, Pallas kernels, body(): pl.pallas_call(functools.partial(kernel, Z, Y, online), out_shape=(jax.Sh...  137 us
    pallas_call x1, Pallas kernels, body(): pl.pallas_call(project, grid=(D // tile,), out_shape=jax.ShapeDtypeStruct...  15 us

profile of v5, /device:TPU:0, one launch (start us, length us, event | category | flops | bytes accessed | tf_op | source)
XLA Modules:
  0.0 152.1 jit_solution(12983659597710666905)
XLA Ops:
  0.0 137.1 %shard_map.55 = (bf16[512,2048]{1,0:T(8,128)(2,1)}, bf16[2048,4096]{1,0:T(8,128)(2,1)}) custom-call(bf16[512,2048]{1,0:T(8,128)(2,1)} %q_ref.1, bf16[4,128,512]{2,1,0:T(8,128)(2,1)} %bitcast.2, bf16[4,128,512]{2,1,0:T(8,128)(2,1)} %bitcast.3, s32[4,8]{1,0:T(4,128)} %t_ref.1, bf16[128,4096]{1,0:T(8,128)(2,1)} %w_ref.1), custom_call_target="tpu_custom_call" | custom-call | flops 4294967296 | bytes 67108864 | tf_op jit(solution)/shard_map/pallas_call | solution.py:471
  137.1 15.0 %shard_map.56 = bf16[512,4096]{1,0:T(8,128)(2,1)} custom-call(bf16[512,2048]{1,0:T(8,128)(2,1)} %get-tuple-element.7.a_ref, bf16[2048,4096]{1,0:T(8,128)(2,1)} %get-tuple-element.8.w_ref), custom_call_target="tpu_custom_call" | custom-call | flops 8589934592 | bytes 23068672 | tf_op jit(solution)/shard_map/pallas_call | solution.py:500

commit v6 on v3

--- a/solution.py
+++ b/solution.py
@@ -498,7 +498,7 @@
         ),
         cost_estimate=pl.CostEstimate(flops=flops, bytes_accessed=64 * 1024 * 1024, transcendentals=0),
     )(queries, keys.reshape(blocks), values.reshape(blocks), table, out_weight)
-    tile = 512
+    tile = 1024
     return pl.pallas_call(
         project,
         grid=(D // tile,),

time: 151 us -> 149 us (0.987)
  Pallas kernels: 151 us -> 149 us
where the time goes in v6:
time: 149 us
  Pallas kernels  149 us (100%)
    pallas_call x1, Pallas kernels, body(): pl.pallas_call(functools.partial(kernel, Z, Y, online), out_shape=(jax.Sh...  136 us
    pallas_call x1, Pallas kernels, body(): pl.pallas_call(project, grid=(D // tile,), out_shape=jax.ShapeDtypeStruct...  13.5 us

profile of v6, /device:TPU:0, one launch (start us, length us, event | category | flops | bytes accessed | tf_op | source)
XLA Modules:
  0.0 149.2 jit_solution(6138357434768960860)
XLA Ops:
  0.0 135.7 %shard_map.55 = (bf16[512,2048]{1,0:T(8,128)(2,1)}, bf16[2048,4096]{1,0:T(8,128)(2,1)}) custom-call(bf16[512,2048]{1,0:T(8,128)(2,1)} %q_ref.1, bf16[4,128,512]{2,1,0:T(8,128)(2,1)} %bitcast.2, bf16[4,128,512]{2,1,0:T(8,128)(2,1)} %bitcast.3, s32[4,8]{1,0:T(4,128)} %t_ref.1, bf16[128,4096]{1,0:T(8,128)(2,1)} %w_ref.1), custom_call_target="tpu_custom_call" | custom-call | flops 4294967296 | bytes 67108864 | tf_op jit(solution)/shard_map/pallas_call | solution.py:473
  135.7 13.5 %shard_map.56 = bf16[512,4096]{1,0:T(8,128)(2,1)} custom-call(bf16[512,2048]{1,0:T(8,128)(2,1)} %get-tuple-element.7.a_ref, bf16[2048,4096]{1,0:T(8,128)(2,1)} %get-tuple-element.8.w_ref), custom_call_target="tpu_custom_call" | custom-call | flops 8589934592 | bytes 23068672 | tf_op jit(solution)/shard_map/pallas_call | solution.py:502
